TPU v7x, 32 devices: a whole 2x2x4 slice. The times are simulated.
32 devices in a mesh: row: 4 (over y, x), col: 8 (over z, core).
Axes of the slice: x: 2, y: 2, z: 4, core: 2. Of those that a mesh axis runs over, the one named last changes fastest.
Arguments:
- rhs: float32 [1536, 3072], P('row', 'col'), may hold values from -6 to 6
- a_pair: float32 [1536, 6144], P('row', 'col'), may hold values from -0.15625 to 0.15625
- b_pair: float32 [3072, 3072], P('row', 'col'), may hold values from -0.15625 to 0.15625
- u_cay: float32 [1536, 384], P('row'), may hold values from -1 to 1, as said below
- v_cay: float32 [384, 3072], P(None, 'col'), may hold values from -1 to 1, as said below
Outputs:
- solved: float32 [1536, 3072], P('row', 'col')
Inputs may be any that keep to these rules, and one draw needn't show every extreme that they name: `u_cay`: each 384 x 384 block of rows has spectral radius below 1. `v_cay`: each 384 x 384 block of columns has spectral radius below 1.
All inputs are finite; a program needn't handle non-finite values.
Results may differ from a plain program's by a relative error of at most 0.0001.
Values sent between devices are 32-bit elements; how exact they have to be, the bound alone decides.
A program may use at most 64 MiB of HBM per device.

v0:
```python
import functools

import jax
import jax.numpy as jnp
from jax import lax
from jax.experimental import pallas as pl
from jax.experimental.pallas import tpu as pltpu
from jax.sharding import PartitionSpec as P

ITERS = 3
CHUNKS = 6
LEFT_1, ABOVE_1, LEFT_2, ABOVE_2 = range(4)
MESH = pl.DeviceIdType.MESH


def parts(x):
    high = x.astype(jnp.bfloat16)
    low = (x - high.astype(jnp.float32)).astype(jnp.bfloat16)
    return high, low


def as_left(x):
    high, low = parts(x)
    return jnp.concatenate([high, high, low], axis=1)


def as_right(x):
    high, low = parts(x)
    return jnp.concatenate([high, low, high], axis=0)


def product(left_side, right_side):
    return jnp.dot(left_side, right_side, preferred_element_type=jnp.float32)


def kernel(rows, cols, rhs_ref, a_ref, b_ref, u_ref, v_ref, out_ref, held, lefts, rights,
           total, send_sem, recv_sem):
    i, j = lax.axis_index("row"), lax.axis_index("col")
    nb = rhs_ref.shape[0]
    size = nb // CHUNKS
    front = rows - 1
    s = i + j
    on_first, on_second, on_trail = s == front, s == front + 1, s >= front + 2
    place = {"row": (i, rows), "col": (j, cols)}

    barrier = pltpu.get_barrier_semaphore()
    count = jnp.int32(0)
    for axis, (k, n) in place.items():
        for by in (-2, -1, 1, 2):
            there = (k + by >= 0) & (k + by < n)
            count = count + there.astype(jnp.int32)

            @pl.when(there)
            def _():
                pl.semaphore_signal(barrier, inc=1, device_id={axis: k + by}, device_id_type=MESH)

    def flow_axis(flow):
        return "col" if flow in (LEFT_1, LEFT_2) else "row"

    def each_send(flow, holds, is_source, source, c, act):
        axis = flow_axis(flow)
        k, n = place[axis]
        even = lax.rem(k, 2) == 0
        span = pl.ds(pl.multiple_of(c * size, size), size)
        for slot, by in ((1, 2), (0, 1)):
            goes = holds & (k + by < n) & (even if by == 2 else (even | is_source))

            @pl.when(goes)
            def _():
                act(pltpu.make_async_remote_copy(
                    src_ref=source.at[span], dst_ref=held.at[flow, span],
                    send_sem=send_sem.at[flow, slot, c], recv_sem=recv_sem.at[flow, c],
                    device_id={axis: k + by}, device_id_type=MESH))

    def receive(flow, c):
        span = pl.ds(pl.multiple_of(c * size, size), size)
        pltpu.make_async_remote_copy(
            src_ref=held.at[flow, span], dst_ref=held.at[flow, span],
            send_sem=send_sem.at[flow, 0, c], recv_sem=recv_sem.at[flow, c],
            device_id={"row": i}, device_id_type=MESH).wait_recv()

    start = lambda copy: copy.start()
    wait_send = lambda copy: copy.wait_send()
    no = jnp.bool_(False)
    yes = jnp.bool_(True)

    def relay(flows):
        def step(c, carry):
            for flow, valid in flows:
                @pl.when(valid)
                def _():
                    receive(flow, c)
                    each_send(flow, yes, no, held.at[flow], c, start)
            return carry
        lax.fori_loop(0, CHUNKS, step, 0)

    above_1 = j <= front
    above_2 = j <= front + 1

    @pl.when(on_first | on_second)
    def _():
        for source, sides, make in ((u_ref, lefts, as_left), (v_ref, rights, as_right)):
            power = source[...]
            sides[0] = make(power)
            for step in range(1, ITERS):
                if make is as_left:
                    power = product(sides[step - 1], as_right(power))
                else:
                    power = product(as_left(power), sides[step - 1])
                sides[step] = make(power)
        total[...] = rhs_ref[...]

    @pl.when(jnp.logical_not(on_first | on_second))
    def _():
        out_ref[...] = rhs_ref[...]

    @pl.when(on_second)
    def _():
        lefts[ITERS] = as_left(a_ref[:, :nb])
        rights[ITERS] = as_right(b_ref[:nb, :])

    @pl.when(on_trail)
    def _():
        for step in range(2):
            lefts[step] = as_left(a_ref[:, step * nb:(step + 1) * nb])
            rights[step] = as_right(b_ref[step * nb:(step + 1) * nb, :])

    pl.semaphore_wait(barrier, count)

    @pl.when(s > front)
    def _():
        relay(((LEFT_1, yes), (ABOVE_1, above_1)))

    @pl.when(on_second)
    def _():
        total[...] -= product(as_left(held[LEFT_1]), rights[ITERS])

        @pl.when(above_1)
        def _():
            total[...] -= product(lefts[ITERS], as_right(held[ABOVE_1]))

    @pl.when(on_first | on_second)
    def _():
        block = total[...]
        scaled = block + product(lefts[0], as_right(block))
        iterate = 0.5 * (scaled + product(as_left(scaled), rights[0]))
        for step in range(ITERS):
            middle = product(as_left(iterate), rights[step])
            iterate = iterate + product(lefts[step], as_right(middle))
        out_ref[...] = iterate

        def step(c, carry):
            each_send(LEFT_1, on_first, yes, out_ref, c, start)
            each_send(ABOVE_1, on_first, yes, out_ref, c, start)
            each_send(LEFT_2, on_second, yes, out_ref, c, start)
            each_send(ABOVE_2, on_second, yes, out_ref, c, start)
            return carry
        lax.fori_loop(0, CHUNKS, step, 0)

    @pl.when(on_trail)
    def _():
        total[...] = product(as_left(held[LEFT_1]), rights[0])

        @pl.when(above_1)
        def _():
            total[...] += product(lefts[0], as_right(held[ABOVE_1]))

        relay(((LEFT_2, yes), (ABOVE_2, above_2)))

        total[...] += product(as_left(held[LEFT_2]), rights[1])

        @pl.when(above_2)
        def _():
            total[...] += product(lefts[1], as_right(held[ABOVE_2]))

        out_ref[...] = rhs_ref[...] - total[...]

    def finish(c, carry):
        each_send(LEFT_1, s >= front, on_first, held.at[LEFT_1], c, wait_send)
        each_send(ABOVE_1, (s >= front) & above_1, on_first, held.at[ABOVE_1], c, wait_send)
        each_send(LEFT_2, s >= front + 1, on_second, held.at[LEFT_2], c, wait_send)
        each_send(ABOVE_2, (s >= front + 1) & above_2, on_second, held.at[ABOVE_2], c, wait_send)
        return carry
    lax.fori_loop(0, CHUNKS, finish, 0)


def body(rows, cols, rhs, a_pair, b_pair, u_cay, v_cay):
    nb = rhs.shape[0]
    return pl.pallas_call(
        functools.partial(kernel, rows, cols),
        out_shape=jax.ShapeDtypeStruct(rhs.shape, jnp.float32),
        in_specs=[pl.BlockSpec(memory_space=pltpu.VMEM)] * 5,
        out_specs=pl.BlockSpec(memory_space=pltpu.VMEM),
        scratch_shapes=[
            pltpu.VMEM((4, nb, nb), jnp.float32),
            pltpu.VMEM((ITERS + 1, nb, 3 * nb), jnp.bfloat16),
            pltpu.VMEM((ITERS + 1, 3 * nb, nb), jnp.bfloat16),
            pltpu.VMEM((nb, nb), jnp.float32),
            pltpu.SemaphoreType.DMA((4, 2, CHUNKS)),
            pltpu.SemaphoreType.DMA((4, CHUNKS)),
        ],
        compiler_params=pltpu.CompilerParams(
            collective_id=0, has_side_effects=True, vmem_limit_bytes=40 * 2**20
        ),
    )(rhs, a_pair, b_pair, u_cay, v_cay)


def solution(mesh):
    placed = (P("row", "col"), P("row", "col"), P("row", "col"), P("row", None), P(None, "col"))
    return jax.shard_map(
        functools.partial(body, mesh.shape["row"], mesh.shape["col"]),
        mesh=mesh, in_specs=placed, out_specs=P("row", "col"), check_vma=False,
    )
```

profile of v0, /device:TPU:31, one launch (start us, length us, event | category | flops | bytes accessed | tf_op | source)
XLA Modules:
  0.0 51.0 jit_solution(11556399775322665434)
XLA Ops:
  0.0 0.0 copy-start
  0.0 1.3 %copy-done = f32[384,768]{1,0:T(8,128)S(1)} copy-done((f32[384,768]{1,0:T(8,128)S(1)}, f32[384,768]{1,0:T(8,128)}, u32[]{:S(2)}) %copy-start) | copy-done | bytes 1179672
  1.3 0.0 copy-start.1
  1.3 1.3 %copy-done.1 = f32[768,384]{1,0:T(8,128)S(1)} copy-done((f32[768,384]{1,0:T(8,128)S(1)}, f32[768,384]{1,0:T(8,128)}, u32[]{:S(2)}) %copy-start.1) | copy-done | bytes 1179672
  2.5 0.0 copy-start.2
  2.5 1.1 %copy-done.2 = f32[384,384]{1,0:T(8,128)S(1)} copy-done((f32[384,384]{1,0:T(8,128)S(1)}, f32[384,384]{1,0:T(8,128)}, u32[]{:S(2)}) %copy-start.2) | copy-done | bytes 589848
  3.6 0.0 copy-start.3
  3.6 1.1 %copy-done.3 = f32[384,384]{1,0:T(8,128)S(1)} copy-done((f32[384,384]{1,0:T(8,128)S(1)}, f32[384,384]{1,0:T(8,128)}, u32[]{:S(2)}) %copy-start.3) | copy-done | bytes 589848
  4.7 0.0 copy-start.4
  4.7 1.1 %copy-done.4 = f32[384,384]{1,0:T(8,128)S(1)} copy-done((f32[384,384]{1,0:T(8,128)S(1)}, f32[384,384]{1,0:T(8,128)}, u32[]{:S(2)}) %copy-start.4) | copy-done | bytes 589848
  5.7 44.4 %shard_map.55 = f32[384,384]{1,0:T(8,128)S(1)} custom-call(f32[384,384]{1,0:T(8,128)S(1)} %copy-done.2, f32[384,768]{1,0:T(8,128)S(1)} %copy-done, f32[768,384]{1,0:T(8,128)S(1)} %copy-done.1, f32[384,384]{1,0:T(8,128)S(1)} %copy-done.3, f32[384,384]{1,0:T(8,128)S(1)} %copy-done.4), custom_call_target="tpu_custom_call" | custom-call | tf_op jit(solution)/shard_map/pallas_call | solution.py:189
  50.2 0.8 %copy.7 = f32[384,384]{1,0:T(8,128)} copy(f32[384,384]{1,0:T(8,128)S(1)} %shard_map.55) | data formatting | bytes 1179648
Async XLA Ops:
  0.0 1.3 %copy-start = (f32[384,768]{1,0:T(8,128)S(1)}, f32[384,768]{1,0:T(8,128)}, u32[]{:S(2)}) copy-start(f32[384,768]{1,0:T(8,128)} %a_ref.1) | copy-start | bytes 3538948
  1.3 1.3 %copy-start.1 = (f32[768,384]{1,0:T(8,128)S(1)}, f32[768,384]{1,0:T(8,128)}, u32[]{:S(2)}) copy-start(f32[768,384]{1,0:T(8,128)} %b_ref.1) | copy-start | bytes 3538948
  2.5 1.1 %copy-start.2 = (f32[384,384]{1,0:T(8,128)S(1)}, f32[384,384]{1,0:T(8,128)}, u32[]{:S(2)}) copy-start(f32[384,384]{1,0:T(8,128)} %rhs_ref.1) | copy-start | bytes 1769476
  3.6 1.1 %copy-start.3 = (f32[384,384]{1,0:T(8,128)S(1)}, f32[384,384]{1,0:T(8,128)}, u32[]{:S(2)}) copy-start(f32[384,384]{1,0:T(8,128)} %u_ref.1) | copy-start | bytes 1769476
  4.7 1.1 %copy-start.4 = (f32[384,384]{1,0:T(8,128)S(1)}, f32[384,384]{1,0:T(8,128)}, u32[]{:S(2)}) copy-start(f32[384,384]{1,0:T(8,128)} %v_ref.1) | copy-start | bytes 1769476
where the time goes:
time: 51.3 us; the launch traced here: 51 us
  Pallas kernels  44.4 us (87%)
  local copies, waits for them, and re-layouts  6.55 us (13%)
    pallas_call x1, Pallas kernels, body(): pl.pallas_call(functools.partial(kernel, rows, cols), out_shape=jax.Shape...  44.4 us
    unnamed x11, local copies, waits for them, and re-layouts  6.55 us

commit v1 on v0

--- a/solution.py
+++ b/solution.py
@@ -9,6 +9,7 @@
 
 ITERS = 3
 CHUNKS = 6
+PIECES = 3
 LEFT_1, ABOVE_1, LEFT_2, ABOVE_2 = range(4)
 MESH = pl.DeviceIdType.MESH
 
@@ -33,8 +34,8 @@
     return jnp.dot(left_side, right_side, preferred_element_type=jnp.float32)
 
 
-def kernel(rows, cols, rhs_ref, a_ref, b_ref, u_ref, v_ref, out_ref, held, lefts, rights,
-           total, send_sem, recv_sem):
+def kernel(rows, cols, rhs_in, a_in, b_in, u_in, v_in, out_ref, rhs_ref, a_ref, b_ref, u_ref,
+           v_ref, held, lefts, rights, total, send_sem, recv_sem, load_sem):
     i, j = lax.axis_index("row"), lax.axis_index("col")
     nb = rhs_ref.shape[0]
     size = nb // CHUNKS
@@ -42,6 +43,32 @@
     s = i + j
     on_first, on_second, on_trail = s == front, s == front + 1, s >= front + 2
     place = {"row": (i, rows), "col": (j, cols)}
+    on_front = on_first | on_second
+
+    def load(which, act):
+        origin, target = (
+            (u_in, u_ref), (v_in, v_ref), (rhs_in, rhs_ref), (a_in, a_ref), (b_in, b_ref)
+        )[which]
+        depth = origin.shape[0] // PIECES
+        for piece in range(PIECES):
+            span = pl.ds(piece * depth, depth)
+            act(pltpu.make_async_copy(
+                origin.at[span], target.at[span], load_sem.at[which, piece]))
+
+    start = lambda copy: copy.start()
+    wait = lambda copy: copy.wait()
+
+    @pl.when(on_front)
+    def _():
+        load(0, start)
+        load(1, start)
+
+    load(2, start)
+
+    @pl.when(s > front)
+    def _():
+        load(3, start)
+        load(4, start)
 
     barrier = pltpu.get_barrier_semaphore()
     count = jnp.int32(0)
@@ -57,12 +84,17 @@
     def flow_axis(flow):
         return "col" if flow in (LEFT_1, LEFT_2) else "row"
 
-    def each_send(flow, holds, is_source, source, c, act):
+    def forwards(flow):
+        k, n = place[flow_axis(flow)]
+        return (lax.rem(k, 2) == 0) & (k + 1 < n)
+
+    def each_send(flow, holds, is_source, source, c, act, hops=(2, 1)):
         axis = flow_axis(flow)
         k, n = place[axis]
         even = lax.rem(k, 2) == 0
         span = pl.ds(pl.multiple_of(c * size, size), size)
-        for slot, by in ((1, 2), (0, 1)):
+        for by in hops:
+            slot = by - 1
             goes = holds & (k + by < n) & (even if by == 2 else (even | is_source))
 
             @pl.when(goes)
@@ -79,7 +111,6 @@
             send_sem=send_sem.at[flow, 0, c], recv_sem=recv_sem.at[flow, c],
             device_id={"row": i}, device_id_type=MESH).wait_recv()
 
-    start = lambda copy: copy.start()
     wait_send = lambda copy: copy.wait_send()
     no = jnp.bool_(False)
     yes = jnp.bool_(True)
@@ -87,19 +118,30 @@
     def relay(flows):
         def step(c, carry):
             for flow, valid in flows:
-                @pl.when(valid)
+                @pl.when(valid & forwards(flow))
                 def _():
                     receive(flow, c)
                     each_send(flow, yes, no, held.at[flow], c, start)
             return carry
         lax.fori_loop(0, CHUNKS, step, 0)
 
+    def collect(flow, valid):
+        @pl.when(valid & jnp.logical_not(forwards(flow)))
+        def _():
+            def step(c, carry):
+                receive(flow, c)
+                return carry
+            lax.fori_loop(0, CHUNKS, step, 0)
+
     above_1 = j <= front
     above_2 = j <= front + 1
 
-    @pl.when(on_first | on_second)
-    def _():
-        for source, sides, make in ((u_ref, lefts, as_left), (v_ref, rights, as_right)):
+    @pl.when(on_front)
+    def _():
+        for which, source, sides, make in (
+            (0, u_ref, lefts, as_left), (1, v_ref, rights, as_right)
+        ):
+            load(which, wait)
             power = source[...]
             sides[0] = make(power)
             for step in range(1, ITERS):
@@ -108,11 +150,21 @@
                 else:
                     power = product(as_left(power), sides[step - 1])
                 sides[step] = make(power)
+
+    load(2, wait)
+
+    @pl.when(on_front)
+    def _():
         total[...] = rhs_ref[...]
 
-    @pl.when(jnp.logical_not(on_first | on_second))
+    @pl.when(s < front)
     def _():
         out_ref[...] = rhs_ref[...]
+
+    @pl.when(s > front)
+    def _():
+        load(3, wait)
+        load(4, wait)
 
     @pl.when(on_second)
     def _():
@@ -130,6 +182,8 @@
     @pl.when(s > front)
     def _():
         relay(((LEFT_1, yes), (ABOVE_1, above_1)))
+        collect(LEFT_1, yes)
+        collect(ABOVE_1, above_1)
 
     @pl.when(on_second)
     def _():
@@ -139,7 +193,7 @@
         def _():
             total[...] -= product(lefts[ITERS], as_right(held[ABOVE_1]))
 
-    @pl.when(on_first | on_second)
+    @pl.when(on_front)
     def _():
         block = total[...]
         scaled = block + product(lefts[0], as_right(block))
@@ -151,12 +205,24 @@
 
         def step(c, carry):
             each_send(LEFT_1, on_first, yes, out_ref, c, start)
-            each_send(ABOVE_1, on_first, yes, out_ref, c, start)
+            each_send(ABOVE_1, on_first, yes, out_ref, c, start, (1,))
             each_send(LEFT_2, on_second, yes, out_ref, c, start)
             each_send(ABOVE_2, on_second, yes, out_ref, c, start)
             return carry
         lax.fori_loop(0, CHUNKS, step, 0)
 
+        @pl.when(on_first)
+        def _():
+            def urgent(c, carry):
+                each_send(ABOVE_1, yes, yes, out_ref, c, wait_send, (1,))
+                return carry
+            lax.fori_loop(0, CHUNKS, urgent, 0)
+
+            def later(c, carry):
+                each_send(ABOVE_1, yes, yes, out_ref, c, start, (2,))
+                return carry
+            lax.fori_loop(0, CHUNKS, later, 0)
+
     @pl.when(on_trail)
     def _():
         total[...] = product(as_left(held[LEFT_1]), rights[0])
@@ -166,8 +232,10 @@
             total[...] += product(lefts[0], as_right(held[ABOVE_1]))
 
         relay(((LEFT_2, yes), (ABOVE_2, above_2)))
+        collect(LEFT_2, yes)
 
         total[...] += product(as_left(held[LEFT_2]), rights[1])
+        collect(ABOVE_2, above_2)
 
         @pl.when(above_2)
         def _():
@@ -177,7 +245,8 @@
 
     def finish(c, carry):
         each_send(LEFT_1, s >= front, on_first, held.at[LEFT_1], c, wait_send)
-        each_send(ABOVE_1, (s >= front) & above_1, on_first, held.at[ABOVE_1], c, wait_send)
+        each_send(ABOVE_1, (s > front) & above_1, no, held.at[ABOVE_1], c, wait_send)
+        each_send(ABOVE_1, on_first, yes, held.at[ABOVE_1], c, wait_send, (2,))
         each_send(LEFT_2, s >= front + 1, on_second, held.at[LEFT_2], c, wait_send)
         each_send(ABOVE_2, (s >= front + 1) & above_2, on_second, held.at[ABOVE_2], c, wait_send)
         return carry
@@ -189,18 +258,24 @@
     return pl.pallas_call(
         functools.partial(kernel, rows, cols),
         out_shape=jax.ShapeDtypeStruct(rhs.shape, jnp.float32),
-        in_specs=[pl.BlockSpec(memory_space=pltpu.VMEM)] * 5,
+        in_specs=[pl.BlockSpec(memory_space=pltpu.HBM)] * 5,
         out_specs=pl.BlockSpec(memory_space=pltpu.VMEM),
         scratch_shapes=[
+            pltpu.VMEM(rhs.shape, jnp.float32),
+            pltpu.VMEM(a_pair.shape, jnp.float32),
+            pltpu.VMEM(b_pair.shape, jnp.float32),
+            pltpu.VMEM(u_cay.shape, jnp.float32),
+            pltpu.VMEM(v_cay.shape, jnp.float32),
             pltpu.VMEM((4, nb, nb), jnp.float32),
             pltpu.VMEM((ITERS + 1, nb, 3 * nb), jnp.bfloat16),
             pltpu.VMEM((ITERS + 1, 3 * nb, nb), jnp.bfloat16),
             pltpu.VMEM((nb, nb), jnp.float32),
             pltpu.SemaphoreType.DMA((4, 2, CHUNKS)),
             pltpu.SemaphoreType.DMA((4, CHUNKS)),
+            pltpu.SemaphoreType.DMA((5, PIECES)),
         ],
         compiler_params=pltpu.CompilerParams(
-            collective_id=0, has_side_effects=True, vmem_limit_bytes=40 * 2**20
+            collective_id=0, has_side_effects=True, vmem_limit_bytes=62 * 2**20
         ),
     )(rhs, a_pair, b_pair, u_cay, v_cay)
 

time: 51.3 us -> 44.8 us (0.87)
  the two profiles are of different devices: /device:TPU:31 before, /device:TPU:15 now
where the time goes in v1:
time: 44.8 us; the launch traced here: 44.6 us
  Pallas kernels  42.7 us (95%)
  local copies, waits for them, and re-layouts  1.92 us (4%)
    pallas_call x1, Pallas kernels, body(): pl.pallas_call(functools.partial(kernel, rows, cols), out_shape=jax.Shape...  42.7 us
    unnamed x1, local copies, waits for them, and re-layouts  1.92 us

profile of v1, /device:TPU:15, one launch (start us, length us, event | category | flops | bytes accessed | tf_op | source)
XLA Modules:
  0.0 44.6 jit_solution(9482161138005912336)
XLA Ops:
  0.0 42.7 %shard_map.55 = f32[384,384]{1,0:T(8,128)} custom-call(f32[384,384]{1,0:T(8,128)} %rhs_in.1, f32[384,768]{1,0:T(8,128)} %a_in.1, f32[768,384]{1,0:T(8,128)} %b_in.1, f32[384,384]{1,0:T(8,128)} %u_in.1, f32[384,384]{1,0:T(8,128)} %v_in.1), custom_call_target="tpu_custom_call" | custom-call | tf_op jit(solution)/shard_map/pallas_call | solution.py:258
  42.7 1.9 %copy.7 = f32[384,384]{1,0:T(8,128)} copy(f32[384,384]{1,0:T(8,128)} %shard_map.55) | data formatting | bytes 1179648

commit v2 on v1

--- a/solution.py
+++ b/solution.py
@@ -10,6 +10,7 @@
 ITERS = 3
 CHUNKS = 6
 PIECES = 3
+SLABS = 3
 LEFT_1, ABOVE_1, LEFT_2, ABOVE_2 = range(4)
 MESH = pl.DeviceIdType.MESH
 
@@ -84,20 +85,29 @@
     def flow_axis(flow):
         return "col" if flow in (LEFT_1, LEFT_2) else "row"
 
-    def forwards(flow):
-        k, n = place[flow_axis(flow)]
-        return (lax.rem(k, 2) == 0) & (k + 1 < n)
-
-    def each_send(flow, holds, is_source, source, c, act, hops=(2, 1)):
+    def hops(flow):
         axis = flow_axis(flow)
         k, n = place[axis]
         even = lax.rem(k, 2) == 0
+        source = front + (flow in (LEFT_2, ABOVE_2)) - (i if axis == "col" else j)
+        if axis == "col":
+            return (1, (k + 1 < n) & (even | (k == source))), (2, (k + 2 < n) & even)
+        odd_source = (source & 1) == 1
+        return (
+            (1, (k + 1 < n) & even & (k != source + 1)),
+            (2, (k + 2 < n) & (even | (k == source))),
+            (-1, odd_source & (k == source + 2)),
+        )
+
+    def forwards(flow):
+        return functools.reduce(jnp.logical_or, [goes for _, goes in hops(flow)])
+
+    def each_send(flow, holds, source, c, act):
+        axis = flow_axis(flow)
+        k, _ = place[axis]
         span = pl.ds(pl.multiple_of(c * size, size), size)
-        for by in hops:
-            slot = by - 1
-            goes = holds & (k + by < n) & (even if by == 2 else (even | is_source))
-
-            @pl.when(goes)
+        for slot, (by, goes) in enumerate(hops(flow)):
+            @pl.when(holds & goes)
             def _():
                 act(pltpu.make_async_remote_copy(
                     src_ref=source.at[span], dst_ref=held.at[flow, span],
@@ -112,7 +122,6 @@
             device_id={"row": i}, device_id_type=MESH).wait_recv()
 
     wait_send = lambda copy: copy.wait_send()
-    no = jnp.bool_(False)
     yes = jnp.bool_(True)
 
     def relay(flows):
@@ -121,7 +130,7 @@
                 @pl.when(valid & forwards(flow))
                 def _():
                     receive(flow, c)
-                    each_send(flow, yes, no, held.at[flow], c, start)
+                    each_send(flow, yes, held.at[flow], c, start)
             return carry
         lax.fori_loop(0, CHUNKS, step, 0)
 
@@ -181,7 +190,7 @@
 
     @pl.when(s > front)
     def _():
-        relay(((LEFT_1, yes), (ABOVE_1, above_1)))
+        relay(((ABOVE_1, above_1), (LEFT_1, yes)))
         collect(LEFT_1, yes)
         collect(ABOVE_1, above_1)
 
@@ -198,30 +207,25 @@
         block = total[...]
         scaled = block + product(lefts[0], as_right(block))
         iterate = 0.5 * (scaled + product(as_left(scaled), rights[0]))
-        for step in range(ITERS):
+        for step in range(ITERS - 1):
             middle = product(as_left(iterate), rights[step])
             iterate = iterate + product(lefts[step], as_right(middle))
-        out_ref[...] = iterate
-
-        def step(c, carry):
-            each_send(LEFT_1, on_first, yes, out_ref, c, start)
-            each_send(ABOVE_1, on_first, yes, out_ref, c, start, (1,))
-            each_send(LEFT_2, on_second, yes, out_ref, c, start)
-            each_send(ABOVE_2, on_second, yes, out_ref, c, start)
+        total[...] = iterate
+        rights[ITERS] = as_right(product(as_left(iterate), rights[ITERS - 1]))
+
+        def send(c, carry):
+            each_send(ABOVE_1, on_first, out_ref, c, start)
+            each_send(LEFT_1, on_first, out_ref, c, start)
+            each_send(LEFT_2, on_second, out_ref, c, start)
+            each_send(ABOVE_2, on_second, out_ref, c, start)
             return carry
-        lax.fori_loop(0, CHUNKS, step, 0)
-
-        @pl.when(on_first)
-        def _():
-            def urgent(c, carry):
-                each_send(ABOVE_1, yes, yes, out_ref, c, wait_send, (1,))
-                return carry
-            lax.fori_loop(0, CHUNKS, urgent, 0)
-
-            def later(c, carry):
-                each_send(ABOVE_1, yes, yes, out_ref, c, start, (2,))
-                return carry
-            lax.fori_loop(0, CHUNKS, later, 0)
+
+        depth = nb // SLABS
+        for slab in range(SLABS):
+            span = pl.ds(slab * depth, depth)
+            out_ref[span] = total[span] + product(lefts[ITERS - 1, span], rights[ITERS])
+            each = CHUNKS // SLABS
+            lax.fori_loop(slab * each, (slab + 1) * each, send, 0)
 
     @pl.when(on_trail)
     def _():
@@ -244,11 +248,10 @@
         out_ref[...] = rhs_ref[...] - total[...]
 
     def finish(c, carry):
-        each_send(LEFT_1, s >= front, on_first, held.at[LEFT_1], c, wait_send)
-        each_send(ABOVE_1, (s > front) & above_1, no, held.at[ABOVE_1], c, wait_send)
-        each_send(ABOVE_1, on_first, yes, held.at[ABOVE_1], c, wait_send, (2,))
-        each_send(LEFT_2, s >= front + 1, on_second, held.at[LEFT_2], c, wait_send)
-        each_send(ABOVE_2, (s >= front + 1) & above_2, on_second, held.at[ABOVE_2], c, wait_send)
+        each_send(LEFT_1, s >= front, held.at[LEFT_1], c, wait_send)
+        each_send(ABOVE_1, (s >= front) & above_1, held.at[ABOVE_1], c, wait_send)
+        each_send(LEFT_2, s >= front + 1, held.at[LEFT_2], c, wait_send)
+        each_send(ABOVE_2, (s >= front + 1) & above_2, held.at[ABOVE_2], c, wait_send)
         return carry
     lax.fori_loop(0, CHUNKS, finish, 0)
 
@@ -270,7 +273,7 @@
             pltpu.VMEM((ITERS + 1, nb, 3 * nb), jnp.bfloat16),
             pltpu.VMEM((ITERS + 1, 3 * nb, nb), jnp.bfloat16),
             pltpu.VMEM((nb, nb), jnp.float32),
-            pltpu.SemaphoreType.DMA((4, 2, CHUNKS)),
+            pltpu.SemaphoreType.DMA((4, 3, CHUNKS)),
             pltpu.SemaphoreType.DMA((4, CHUNKS)),
             pltpu.SemaphoreType.DMA((5, PIECES)),
         ],

time: 44.8 us -> 44.3 us (0.989)
  the two profiles are of different devices: /device:TPU:15 before, /device:TPU:29 now
where the time goes in v2:
time: 44.3 us; the launch traced here: 44.1 us
  Pallas kernels  42.2 us (95%)
  local copies, waits for them, and re-layouts  1.92 us (4%)
    pallas_call x1, Pallas kernels, body(): pl.pallas_call(functools.partial(kernel, rows, cols), out_shape=jax.Shape...  42.2 us
    unnamed x1, local copies, waits for them, and re-layouts  1.92 us

profile of v2, /device:TPU:29, one launch (start us, length us, event | category | flops | bytes accessed | tf_op | source)
XLA Modules:
  0.0 44.1 jit_solution(15757088422820924529)
XLA Ops:
  0.0 42.2 %shard_map.55 = f32[384,384]{1,0:T(8,128)} custom-call(f32[384,384]{1,0:T(8,128)} %rhs_in.1, f32[384,768]{1,0:T(8,128)} %a_in.1, f32[768,384]{1,0:T(8,128)} %b_in.1, f32[384,384]{1,0:T(8,128)} %u_in.1, f32[384,384]{1,0:T(8,128)} %v_in.1), custom_call_target="tpu_custom_call" | custom-call | tf_op jit(solution)/shard_map/pallas_call | solution.py:261
  42.2 1.9 %copy.7 = f32[384,384]{1,0:T(8,128)} copy(f32[384,384]{1,0:T(8,128)} %shard_map.55) | data formatting | bytes 1179648

commit v3 on v2

--- a/solution.py
+++ b/solution.py
@@ -8,7 +8,7 @@
 from jax.sharding import PartitionSpec as P
 
 ITERS = 3
-CHUNKS = 6
+CHUNKS = 12
 PIECES = 3
 SLABS = 3
 LEFT_1, ABOVE_1, LEFT_2, ABOVE_2 = range(4)
@@ -190,7 +190,8 @@
 
     @pl.when(s > front)
     def _():
-        relay(((ABOVE_1, above_1), (LEFT_1, yes)))
+        relay(((ABOVE_1, above_1),))
+        relay(((LEFT_1, yes),))
         collect(LEFT_1, yes)
         collect(ABOVE_1, above_1)
 

time: 44.3 us -> 44.3 us (level)
  no operation moved by 1% of the time
where the time goes in v3:
time: 44.3 us; the launch traced here: 44.1 us
  Pallas kernels  42.2 us (95%)
  local copies, waits for them, and re-layouts  1.92 us (4%)
    pallas_call x1, Pallas kernels, body(): pl.pallas_call(functools.partial(kernel, rows, cols), out_shape=jax.Shape...  42.2 us
    unnamed x1, local copies, waits for them, and re-layouts  1.92 us

profile of v3, /device:TPU:29, one launch (start us, length us, event | category | flops | bytes accessed | tf_op | source)
XLA Modules:
  0.0 44.1 jit_solution(6943264945102718092)
XLA Ops:
  0.0 42.2 %shard_map.55 = f32[384,384]{1,0:T(8,128)} custom-call(f32[384,384]{1,0:T(8,128)} %rhs_in.1, f32[384,768]{1,0:T(8,128)} %a_in.1, f32[768,384]{1,0:T(8,128)} %b_in.1, f32[384,384]{1,0:T(8,128)} %u_in.1, f32[384,384]{1,0:T(8,128)} %v_in.1), custom_call_target="tpu_custom_call" | custom-call | tf_op jit(solution)/shard_map/pallas_call | solution.py:262
  42.2 1.9 %copy.7 = f32[384,384]{1,0:T(8,128)} copy(f32[384,384]{1,0:T(8,128)} %shard_map.55) | data formatting | bytes 1179648

commit v4 on v3

--- a/solution.py
+++ b/solution.py
@@ -8,7 +8,7 @@
 from jax.sharding import PartitionSpec as P
 
 ITERS = 3
-CHUNKS = 12
+CHUNKS = 6
 PIECES = 3
 SLABS = 3
 LEFT_1, ABOVE_1, LEFT_2, ABOVE_2 = range(4)
@@ -134,13 +134,13 @@
             return carry
         lax.fori_loop(0, CHUNKS, step, 0)
 
-    def collect(flow, valid):
+    def collect(flow, valid, first=0, last=CHUNKS):
         @pl.when(valid & jnp.logical_not(forwards(flow)))
         def _():
             def step(c, carry):
                 receive(flow, c)
                 return carry
-            lax.fori_loop(0, CHUNKS, step, 0)
+            lax.fori_loop(first, last, step, 0)
 
     above_1 = j <= front
     above_2 = j <= front + 1
@@ -193,11 +193,17 @@
         relay(((ABOVE_1, above_1),))
         relay(((LEFT_1, yes),))
         collect(LEFT_1, yes)
+
+    @pl.when(on_second)
+    def _():
+        total[...] -= product(as_left(held[LEFT_1]), rights[ITERS])
+
+    @pl.when(s > front)
+    def _():
         collect(ABOVE_1, above_1)
 
     @pl.when(on_second)
     def _():
-        total[...] -= product(as_left(held[LEFT_1]), rights[ITERS])
 
         @pl.when(above_1)
         def _():
@@ -237,9 +243,12 @@
             total[...] += product(lefts[0], as_right(held[ABOVE_1]))
 
         relay(((LEFT_2, yes), (ABOVE_2, above_2)))
-        collect(LEFT_2, yes)
-
-        total[...] += product(as_left(held[LEFT_2]), rights[1])
+        each, depth = CHUNKS // SLABS, nb // SLABS
+        for slab in range(SLABS):
+            collect(LEFT_2, yes, slab * each, (slab + 1) * each)
+            span = pl.ds(slab * depth, depth)
+            total[span] += product(as_left(held[LEFT_2, span]), rights[1])
+
         collect(ABOVE_2, above_2)
 
         @pl.when(above_2)

time: 44.3 us -> 43.4 us (0.980)
  Pallas kernels: 42.2 us -> 41.3 us
    pallas_call x1, Pallas kernels: 42.2 us -> 41.3 us  [body(): pl.pallas_call(functools.partial(kernel, rows, cols), out_shape=jax.Shape...]
where the time goes in v4:
time: 43.4 us; the launch traced here: 43.2 us
  Pallas kernels  41.3 us (95%)
  local copies, waits for them, and re-layouts  1.92 us (4%)
    pallas_call x1, Pallas kernels, body(): pl.pallas_call(functools.partial(kernel, rows, cols), out_shape=jax.Shape...  41.3 us
    unnamed x1, local copies, waits for them, and re-layouts  1.92 us

profile of v4, /device:TPU:29, one launch (start us, length us, event | category | flops | bytes accessed | tf_op | source)
XLA Modules:
  0.0 43.2 jit_solution(2582883710709042943)
XLA Ops:
  0.0 41.3 %shard_map.55 = f32[384,384]{1,0:T(8,128)} custom-call(f32[384,384]{1,0:T(8,128)} %rhs_in.1, f32[384,768]{1,0:T(8,128)} %a_in.1, f32[768,384]{1,0:T(8,128)} %b_in.1, f32[384,384]{1,0:T(8,128)} %u_in.1, f32[384,384]{1,0:T(8,128)} %v_in.1), custom_call_target="tpu_custom_call" | custom-call | tf_op jit(solution)/shard_map/pallas_call | solution.py:271
  41.3 1.9 %copy.7 = f32[384,384]{1,0:T(8,128)} copy(f32[384,384]{1,0:T(8,128)} %shard_map.55) | data formatting | bytes 1179648
